TPU v7x, 32 devices: a whole 2x2x4 slice. The times are simulated.
32 devices in a mesh: dp: 4 (over z), ctx: 8 (over y, x, core).
Axes of the slice: x: 2, y: 2, z: 4, core: 2. Of those that a mesh axis runs over, the one named last changes fastest.
Arguments:
- frames: bfloat16 [4, 1024, 512], P('dp', 'ctx'), may hold values from -6 to 6
- conv_weight: bfloat16 [3, 512, 512], replicated, may hold values from -0.15625 to 0.15625
- proj_weight: bfloat16 [512, 768], replicated, may hold values from -0.25 to 0.25
- query_weight: bfloat16 [768, 384], replicated, may hold values from -1.5 to 1.5
- key_weight: bfloat16 [768, 384], replicated, may hold values from -1.5 to 1.5
- value_weight: bfloat16 [768, 384], replicated, may hold values from -0.21875 to 0.21875
- cotangent: bfloat16 [4, 512, 384], P('dp', 'ctx'), may hold values from -6 to 6
Outputs:
- weight_grad: float32 [1536, 512], P('ctx', 'dp')
- frame_grad: bfloat16 [4, 1024, 512], P('dp', 'ctx')
All inputs are finite; a program needn't handle non-finite values.
Results may differ from a plain program's by a relative error of at most 0.04.
Values may be sent and summed in bfloat16 or wider, within the bound.
A program may use at most 64 MiB of HBM per device.

v0:
```python
import math

import jax
import jax.numpy as jnp
from jax import lax
from jax.sharding import PartitionSpec as P

HEADS = 6
HEAD_DIM = 64


SQRT_HALF = 0.7071067811865476
INV_ROOT_TAU = 0.3989422804014327
EPSILON = 1e-05


def from_behind(value, axis, steps):
    count = lax.axis_size(axis)
    initial, last = (max(0, -steps), min(count, count - steps))
    return lax.ppermute(value, axis, [(source, source + steps) for source in range(initial, last)])


def gelu_slope(pre):
    return 0.5 * (1.0 + lax.erf(pre * SQRT_HALF)) + pre * INV_ROOT_TAU * jnp.exp(-0.5 * pre * pre)


def blocked(step_fn, carry, piece):
    rows = piece[0].shape[0]
    block_rows = math.gcd(rows, 512)
    block_count = rows // block_rows
    stacked = tuple(
        (member.reshape((block_count, block_rows) + member.shape[1:]) for member in piece)
    )

    def inner(state, item):
        block_index, members = item
        return (step_fn(state, members, block_index * block_rows), None)

    final, unused = lax.scan(inner, carry, (jnp.arange(block_count, dtype=jnp.int32), stacked))
    return final


def local(frames, conv_weight, proj_weight, query_weight, key_weight, value_weight, cotangent):
    inputs = frames[0]
    count = inputs.shape[0] // 2
    width = inputs.shape[1]
    following = from_behind(inputs[:1], "ctx", -1)
    paired = inputs.reshape(count, 2, width)
    tap_first = paired[:, 0]
    tap_second = paired[:, 1]
    tap_third = jnp.concatenate([tap_first[1:], following], 0)
    conv_out = jnp.dot(tap_first, conv_weight[0], preferred_element_type=jnp.float32)
    conv_out = conv_out + jnp.dot(tap_second, conv_weight[1], preferred_element_type=jnp.float32)
    conv_out = conv_out + jnp.dot(tap_third, conv_weight[2], preferred_element_type=jnp.float32)
    activated = jax.nn.gelu(conv_out, approximate=False)
    centre = jnp.mean(activated, -1, keepdims=True)
    spread = jnp.mean((activated - centre) ** 2, -1, keepdims=True)
    inv_std = lax.rsqrt(spread + EPSILON)
    normed = (activated - centre) * inv_std
    hidden = jnp.dot(
        normed.astype(jnp.bfloat16), proj_weight, preferred_element_type=jnp.float32
    ).astype(jnp.bfloat16)
    queries = jnp.dot(hidden, query_weight, preferred_element_type=jnp.float32).astype(jnp.bfloat16)
    keys = jnp.dot(hidden, key_weight, preferred_element_type=jnp.float32).astype(jnp.bfloat16)
    values = jnp.dot(hidden, value_weight, preferred_element_type=jnp.float32).astype(jnp.bfloat16)
    upstream = cotangent[0]
    scale = HEAD_DIM ** (-0.5)
    query_heads = queries.reshape(count, HEADS, HEAD_DIM)
    key_heads = keys.reshape(count, HEADS, HEAD_DIM)
    value_heads = values.reshape(count, HEADS, HEAD_DIM)
    grad_heads = upstream.reshape(count, HEADS, HEAD_DIM)

    def forward_block(carry, piece, start):
        running_top, running_total, accum = carry
        rows = piece[0].shape[0]
        keys_part = piece[0].reshape(rows, HEADS, HEAD_DIM)
        values_part = piece[1].reshape(rows, HEADS, HEAD_DIM)
        scores = (
            jnp.einsum("qhe,khe->hqk", query_heads, keys_part, preferred_element_type=jnp.float32)
            * scale
        )
        new_top = jnp.maximum(running_top, jnp.max(scores, -1))
        factor = jnp.exp(running_top - new_top)
        weights = jnp.exp(scores - new_top[:, :, None])
        new_total = running_total * factor + jnp.sum(weights, -1)
        new_accum = accum * jnp.transpose(factor)[:, :, None] + jnp.einsum(
            "hqk,khe->qhe",
            weights,
            values_part.astype(jnp.float32),
            precision=lax.Precision.HIGHEST,
        )
        return (new_top, new_total, new_accum)

    start_state = (
        jnp.full((HEADS, count), -jnp.inf, jnp.float32),
        jnp.zeros((HEADS, count), jnp.float32),
        jnp.zeros((count, HEADS, HEAD_DIM), jnp.float32),
    )
    final_top, final_total, final_accum = blocked(
        forward_block,
        start_state,
        (
            lax.all_gather(keys, "ctx", axis=0, tiled=True),
            lax.all_gather(values, "ctx", axis=0, tiled=True),
        ),
    )
    lse_heads = final_top + jnp.log(final_total)
    outputs = final_accum / jnp.transpose(final_total)[:, :, None]
    delta_rows = jnp.sum(grad_heads.astype(jnp.float32) * outputs, -1)
    delta_heads = jnp.transpose(delta_rows)

    def query_block(carry, piece, start):
        rows = piece[0].shape[0]
        keys_part = piece[0].reshape(rows, HEADS, HEAD_DIM)
        values_part = piece[1].reshape(rows, HEADS, HEAD_DIM)
        scores = (
            jnp.einsum("qhe,khe->hqk", query_heads, keys_part, preferred_element_type=jnp.float32)
            * scale
        )
        probs = jnp.exp(scores - lse_heads[:, :, None])
        prob_grad = jnp.einsum(
            "qhe,khe->hqk", grad_heads, values_part, preferred_element_type=jnp.float32
        )
        score_grad = probs * (prob_grad - delta_heads[:, :, None])
        return carry + jnp.einsum(
            "hqk,khe->qhe",
            score_grad.astype(jnp.bfloat16),
            keys_part,
            preferred_element_type=jnp.float32,
        )

    query_start = jnp.zeros((count, HEADS, HEAD_DIM), jnp.float32)
    query_accum = blocked(
        query_block,
        query_start,
        (
            lax.all_gather(keys, "ctx", axis=0, tiled=True),
            lax.all_gather(values, "ctx", axis=0, tiled=True),
        ),
    )
    query_grad = (query_accum * scale).astype(jnp.bfloat16).reshape(count, HEADS * HEAD_DIM)
    all_lse, all_delta = (
        lax.all_gather(jnp.transpose(lse_heads), "ctx", axis=0, tiled=True),
        lax.all_gather(delta_rows, "ctx", axis=0, tiled=True),
    )

    def key_block(carry, piece, start):
        key_accum, value_accum = carry
        rows = piece[0].shape[0]
        query_part = piece[0].reshape(rows, HEADS, HEAD_DIM)
        grad_part = piece[1].reshape(rows, HEADS, HEAD_DIM)
        lse_part = jnp.transpose(lax.dynamic_slice_in_dim(all_lse, start, rows, 0))
        delta_part = jnp.transpose(lax.dynamic_slice_in_dim(all_delta, start, rows, 0))
        scores = (
            jnp.einsum("qhe,khe->hqk", query_part, key_heads, preferred_element_type=jnp.float32)
            * scale
        )
        probs = jnp.exp(scores - lse_part[:, :, None])
        value_accum = value_accum + jnp.einsum(
            "hqk,qhe->khe",
            probs.astype(jnp.bfloat16),
            grad_part,
            preferred_element_type=jnp.float32,
        )
        prob_grad = jnp.einsum(
            "qhe,khe->hqk", grad_part, value_heads, preferred_element_type=jnp.float32
        )
        score_grad = probs * (prob_grad - delta_part[:, :, None])
        key_accum = key_accum + jnp.einsum(
            "hqk,qhe->khe",
            score_grad.astype(jnp.bfloat16),
            query_part,
            preferred_element_type=jnp.float32,
        )
        return (key_accum, value_accum)

    key_start = (
        jnp.zeros((count, HEADS, HEAD_DIM), jnp.float32),
        jnp.zeros((count, HEADS, HEAD_DIM), jnp.float32),
    )
    key_accum, value_accum = blocked(
        key_block,
        key_start,
        (
            lax.all_gather(queries, "ctx", axis=0, tiled=True),
            lax.all_gather(upstream, "ctx", axis=0, tiled=True),
        ),
    )
    key_grad = (key_accum * scale).astype(jnp.bfloat16).reshape(count, HEADS * HEAD_DIM)
    value_grad = value_accum.astype(jnp.bfloat16).reshape(count, HEADS * HEAD_DIM)
    hidden_grad = jnp.einsum(
        "tk,dk->td", query_grad, query_weight, preferred_element_type=jnp.float32
    )
    hidden_grad = hidden_grad + jnp.einsum(
        "tk,dk->td", key_grad, key_weight, preferred_element_type=jnp.float32
    )
    hidden_grad = hidden_grad + jnp.einsum(
        "tk,dk->td", value_grad, value_weight, preferred_element_type=jnp.float32
    )
    hidden_grad = hidden_grad.astype(jnp.bfloat16)
    normed_grad = jnp.einsum(
        "td,cd->tc", hidden_grad, proj_weight, preferred_element_type=jnp.float32
    )
    act_grad = inv_std * (
        normed_grad
        - jnp.mean(normed_grad, -1, keepdims=True)
        - normed * jnp.mean(normed_grad * normed, -1, keepdims=True)
    )
    conv_grad = (act_grad * gelu_slope(conv_out)).astype(jnp.bfloat16)
    kernel_terms = jnp.concatenate(
        [
            jnp.einsum("tc,to->co", tap_first, conv_grad, preferred_element_type=jnp.float32),
            jnp.einsum("tc,to->co", tap_second, conv_grad, preferred_element_type=jnp.float32),
            jnp.einsum("tc,to->co", tap_third, conv_grad, preferred_element_type=jnp.float32),
        ],
        0,
    )
    earlier = from_behind(conv_grad[count - 1 :], "ctx", 1)
    first = jnp.einsum("to,co->tc", conv_grad, conv_weight[0], preferred_element_type=jnp.float32)
    second = jnp.einsum("to,co->tc", conv_grad, conv_weight[1], preferred_element_type=jnp.float32)
    third = jnp.einsum("to,co->tc", conv_grad, conv_weight[2], preferred_element_type=jnp.float32)
    incoming = jnp.einsum("to,co->tc", earlier, conv_weight[2], preferred_element_type=jnp.float32)
    moved = jnp.concatenate([incoming, third[:-1]], 0)
    even_rows = first + moved
    frame_rows = jnp.stack([even_rows, second], 1).reshape(2 * count, width).astype(jnp.bfloat16)
    frame_sum = lax.psum_scatter(
        kernel_terms.astype(jnp.bfloat16), "ctx", scatter_dimension=0, tiled=True
    )
    weight_grad = lax.psum_scatter(frame_sum, "dp", scatter_dimension=1, tiled=True).astype(
        jnp.float32
    )
    return (weight_grad, frame_rows[None])


def solution(mesh):
    in_specs = (P("dp", "ctx", None), P(), P(), P(), P(), P(), P("dp", "ctx", None))
    out_specs = (P("ctx", "dp"), P("dp", "ctx", None))
    return jax.shard_map(local, mesh=mesh, in_specs=in_specs, out_specs=out_specs, check_vma=False)
```

profile of v0, /device:TPU:1, one launch (start us, length us, event | category | flops | bytes accessed | tf_op | source)
XLA Modules:
  0.0 177.5 jit_solution(5564387920158402411)
XLA Ops:
  8.0 2.0 %collective-permute-start = (bf16[1,512]{1,0:T(2,128)(2,1)S(1)}, bf16[1,512]{1,0:T(2,128)(2,1)S(1)}, u32[]{:S(2)}, u32[]{:S(2)}) collective-permute-start(bf16[1,512]{1,0:T(2,128)(2,1)S(1)} %slice_bitcast_fusion), channel_id=1, source_target_pairs={{1,0},{2,1},{3,2},{4,3},{5,4},{6,5},{7,6},{9,8},{10,9},{11,10},{12... | collective-permute-start | bytes 3080 | tf_op jit(solution)/shard_map/ppermute | solution.py:20
  13.8 11.8 %all-gather = bf16[1,512,384]{2,1,0:T(8,128)(2,1)S(1)} all-gather(bf16[1,64,384]{2,1,0:T(8,128)(2,1)S(1)} %copy-done.17), channel_id=2, replica_groups=mesh['dp'=4,'ctx'=8] {'ctx'}, dimensions={1}, use_global_device_ids=true | all-gather | bytes 442368 | tf_op jit(solution)/shard_map/all_gather | solution.py:186
  30.6 9.7 %all_gather.20 = bf16[512,384]{1,0:T(8,128)(2,1)} all-gather(bf16[64,384]{1,0:T(8,128)(2,1)S(1)} %convolution_convert_fusion.8), channel_id=1, replica_groups=mesh['dp'=4,'ctx'=8] {'ctx'}, dimensions={0}, use_global_device_ids=true | all-gather | bytes 442368 | tf_op jit(solution)/shard_map/all_gather | solution.py:137
  40.2 1.9 %copy.38 = bf16[512,384]{0,1:T(8,128)(2,1)} copy(bf16[512,384]{1,0:T(8,128)(2,1)} %all_gather.20) | data formatting | bytes 786432 | tf_op jit(solution)/shard_map/all_gather | solution.py:137
  43.2 1.4 fusion.93
  45.4 10.4 %all_gather.22 = bf16[512,384]{1,0:T(8,128)(2,1)} all-gather(bf16[64,384]{1,0:T(8,128)(2,1)S(1)} %copy-done.13), channel_id=1, replica_groups=mesh['dp'=4,'ctx'=8] {'ctx'}, dimensions={0}, use_global_device_ids=true | all-gather | bytes 442368 | tf_op jit(solution)/shard_map/all_gather | solution.py:185
  55.9 1.6 reshape.119
  59.4 9.7 %all_gather.21 = bf16[512,384]{1,0:T(8,128)(2,1)} all-gather(bf16[64,384]{1,0:T(8,128)(2,1)S(1)} %convolution_convert_fusion.6), channel_id=1, replica_groups=mesh['dp'=4,'ctx'=8] {'ctx'}, dimensions={0}, use_global_device_ids=true | all-gather | bytes 442368 | tf_op jit(solution)/shard_map/all_gather | solution.py:138
  69.1 1.6 reshape.120
  70.7 1.9 %copy.40 = bf16[512,384]{0,1:T(8,128)(2,1)} copy(bf16[512,384]{1,0:T(8,128)(2,1)} %all_gather.21) | data formatting | bytes 786432 | tf_op jit(solution)/shard_map/all_gather | solution.py:138
  72.6 1.7 fusion.20
  74.3 2.3 %fusion.19 = bf16[6,64,64]{2,1,0:T(8,128)(2,1)} fusion(bf16[512,6,64]{0,2,1:T(8,128)(2,1)} %bitcast.157, bf16[512,6,64]{0,2,1:T(8,128)(2,1)} %bitcast.161, bf16[64,6,64]{0,2,1:T(8,128)(2,1)} %bitcast.166, f32[6,64,512]{2,1,0:T(8,128)S(1)} %get-tuple-element.67, f32[6,64]{1,0:T(8,128)S(1)} %bitcast.170, f32[6,64]{1,0:T(8,128)S(1)} %log_add_fusion), kind=kOutput, calls=%fused_computation.30 | convolution fusion | flops 51167232 | bytes 1674240 | tf_op jit(solution)/shard_map/while/body/eval_jaxpr/hqk,khe->qhe/dot_general | solution.py:125
  76.6 2.1 %fusion.96 = f32[64,768]{1,0:T(8,128)} fusion(bf16[64,384]{0,1:T(8,128)(2,1)} %bitcast.164, bf16[768,384]{1,0:T(8,128)(2,1)} %param.10), kind=kOutput, calls=%fused_computation.137 | convolution fusion | flops 37748736 | bytes 835584 | tf_op jit(solution)/shard_map/tk,dk->td/dot_general | solution.py:191
  78.7 1.9 %copy.43 = bf16[512,384]{0,1:T(8,128)(2,1)} copy(bf16[512,384]{1,0:T(8,128)(2,1)} %all_gather.22) | data formatting | bytes 786432 | tf_op jit(solution)/shard_map/all_gather | solution.py:185
  80.6 8.9 %all-gather.1 = f32[8,64,6]{1,2,0:T(8,128)S(1)} all-gather(f32[1,64,6]{1,2,0:T(8,128)S(1)} %get-tuple-element.62), channel_id=1, replica_groups=mesh['dp'=4,'ctx'=8] {'ctx'}, dimensions={0}, use_global_device_ids=true | all-gather | bytes 13824 | tf_op jit(solution)/shard_map/all_gather | solution.py:143
  90.2 8.2 %all-gather.2 = f32[8,64,6]{1,2,0:T(8,128)S(1)} all-gather(f32[1,64,6]{1,2,0:T(8,128)S(1)} %bitcast.171), channel_id=1, replica_groups=mesh['dp'=4,'ctx'=8] {'ctx'}, dimensions={0}, use_global_device_ids=true | all-gather | bytes 13824 | tf_op jit(solution)/shard_map/all_gather | solution.py:144
  100.8 1.7 reshape.123
  102.4 2.1 %fusion.18 = bf16[6,64,64]{2,1,0:T(8,128)(2,1)} fusion(bf16[512,6,64]{0,2,1:T(8,128)(2,1)} %bitcast.155, f32[6,512,64]{1,2,0:T(8,128)S(1)} %fusion.1, bf16[512,6,64]{0,2,1:T(8,128)(2,1)S(1)} %bitcast.153, f32[6,512]{1,0:T(8,128)S(1)} %bitcast.167, bf16[64,6,64]{2,1,0:T(8,128)(2,1)} %reshape.120), kind=kOutput, calls=%fused_computation.29 | convolution fusion | flops 50970624 | bytes 1683456 | tf_op jit(solution)/shard_map/while/body/eval_jaxpr/hqk,qhe->khe/dot_general | solution.py:169
  104.5 1.5 convolution_add_fusion.1
  106.0 1.8 fusion.89
  110.4 3.1 %collective-permute-start.1 = (bf16[1,512]{1,0:T(2,128)(2,1)S(1)}, bf16[1,512]{1,0:T(2,128)(2,1)S(1)}, u32[]{:S(2)}, u32[]{:S(2)}) collective-permute-start(bf16[1,512]{1,0:T(2,128)(2,1)S(1)} %slice.53), channel_id=1, source_target_pairs={{0,1},{1,2},{2,3},{3,4},{4,5},{5,6},{6,7},{8,9},{9,10},{10,11},{11... | collective-permute-start | bytes 3080 | tf_op jit(solution)/shard_map/ppermute | solution.py:20
  114.1 34.7 %reduce-scatter.5.cloned.1.call-done = bf16[192,512]{1,0:T(8,128)(2,1)} async-done(((bf16[1536,512]{1,0:T(8,128)(2,1)}), bf16[192,512]{1,0:T(8,128)(2,1)}) %reduce-scatter.5.cloned.1.call-update) | async-done | bytes 196624 | tf_op jit(solution)/shard_map/reduce_scatter | solution.py:226
  148.7 1.8 copy.52
  151.9 17.1 %reduce-scatter.7.cloned.1.call-done = bf16[128,192]{1,0:T(8,128)(2,1)} async-done(((bf16[512,192]{1,0:T(8,128)(2,1)}), bf16[128,192]{1,0:T(8,128)(2,1)}) %reduce-scatter.7.cloned.1.call-update) | async-done | bytes 49168
  (100 shorter events, 22.4 us)
Async XLA Ops:
  7.2 22.2 %copy-start = (bf16[512,768]{1,0:T(8,128)(2,1)S(1)}, bf16[512,768]{1,0:T(8,128)(2,1)}, u32[]{:S(2)}) copy-start(bf16[512,768]{1,0:T(8,128)(2,1)} %param.9) | copy-start | bytes 2359300
  7.2 6.6 %copy-start.17 = (bf16[1,64,384]{2,1,0:T(8,128)(2,1)S(1)}, bf16[1,64,384]{2,1,0:T(8,128)(2,1)}, u32[]{:S(2)}) copy-start(bf16[1,64,384]{2,1,0:T(8,128)(2,1)} %param.13) | copy-start | bytes 147460
  7.2 141.5 %reduce-scatter.5.cloned.1.call-start = ((), (), s32[]{:S(2)}) async-start(), calls=%async_computation.2 | async-start | bytes 1769472 | tf_op jit(solution)/shard_map/reduce_scatter | solution.py:226
  8.0 18.6 %collective-permute-start = (bf16[1,512]{1,0:T(2,128)(2,1)S(1)}, bf16[1,512]{1,0:T(2,128)(2,1)S(1)}, u32[]{:S(2)}, u32[]{:S(2)}) collective-permute-start(bf16[1,512]{1,0:T(2,128)(2,1)S(1)} %slice_bitcast_fusion), channel_id=1, source_target_pairs={{1,0},{2,1},{3,2},{4,3},{5,4},{6,5},{7,6},{9,8},{10,9},{11,10},{12... | collective-permute-start | bytes 3080 | tf_op jit(solution)/shard_map/ppermute | solution.py:20
  11.1 1.4 copy-start.7
  11.1 2.7 %copy-start.9 = (bf16[64,1,512]{2,1,0:T(2,128)(2,1)}, bf16[64,1,512]{2,1,0:T(2,128)(2,1)S(1)}, u32[]{:S(2)}) copy-start(bf16[64,1,512]{2,1,0:T(2,128)(2,1)S(1)} %get-tuple-element.60) | copy-start | bytes 196612
  11.1 15.9 %copy-start.1 = (bf16[3,512,512]{2,1,0:T(8,128)(2,1)S(1)}, bf16[3,512,512]{2,1,0:T(8,128)(2,1)}, u32[]{:S(2)}) copy-start(bf16[3,512,512]{2,1,0:T(8,128)(2,1)} %param.8) | copy-start | bytes 4718596
  26.6 1.6 copy-start.23
  27.1 2.6 %copy-start.3 = (bf16[768,384]{1,0:T(8,128)(2,1)S(1)}, bf16[768,384]{1,0:T(8,128)(2,1)}, u32[]{:S(2)}) copy-start(bf16[768,384]{1,0:T(8,128)(2,1)} %param.11) | copy-start | bytes 1769476
  28.3 1.7 copy-start.4
  28.3 13.9 %copy-start.2 = (bf16[768,384]{1,0:T(8,128)(2,1)S(1)}, bf16[768,384]{1,0:T(8,128)(2,1)}, u32[]{:S(2)}) copy-start(bf16[768,384]{1,0:T(8,128)(2,1)} %param.10) | copy-start | bytes 1769476
  29.7 13.5 %copy-start.6 = (bf16[64,768]{1,0:T(8,128)(2,1)}, bf16[64,768]{1,0:T(8,128)(2,1)S(1)}, u32[]{:S(2)}) copy-start(bf16[64,768]{1,0:T(8,128)(2,1)S(1)} %convolution_convert_fusion.4) | copy-start | bytes 294916
  42.4 0.8 copy-start.12
  43.2 2.3 %copy-start.13 = (bf16[64,384]{1,0:T(8,128)(2,1)S(1)}, bf16[64,384]{1,0:T(8,128)(2,1)}, u32[]{:S(2)}) copy-start(bf16[64,384]{1,0:T(8,128)(2,1)} %copy-done.12) | copy-start | bytes 147460
  104.5 3.3 %copy-start.5 = (f32[64,512]{1,0:T(8,128)S(1)}, f32[64,512]{1,0:T(8,128)}, u32[]{:S(2)}) copy-start(f32[64,512]{1,0:T(8,128)} %copy-done.4) | copy-start | bytes 393220
  104.5 3.3 %copy-start.18 = (f32[64,512]{1,0:T(8,128)S(1)}, f32[64,512]{1,0:T(8,128)}, u32[]{:S(2)}) copy-start(f32[64,512]{1,0:T(8,128)} %get-tuple-element.65) | copy-start | bytes 393220
  104.5 3.4 %copy-start.20 = (f32[64]{0:T(128)S(1)}, f32[64]{0:T(128)}, u32[]{:S(2)}) copy-start(f32[64]{0:T(128)} %copy-done.19) | copy-start | bytes 772
  104.5 3.4 %copy-start.22 = (f32[64]{0:T(128)S(1)}, f32[64]{0:T(128)}, u32[]{:S(2)}) copy-start(f32[64]{0:T(128)} %copy-done.21) | copy-start | bytes 772
  104.5 3.5 %copy-start.10 = (bf16[64,1,512]{2,1,0:T(2,128)(2,1)S(1)}, bf16[64,1,512]{2,1,0:T(2,128)(2,1)}, u32[]{:S(2)}) copy-start(bf16[64,1,512]{2,1,0:T(2,128)(2,1)} %copy-done.9) | copy-start | bytes 196612
  106.0 2.3 %copy-start.8 = (bf16[64,1,512]{2,1,0:T(2,128)(2,1)S(1)}, bf16[64,1,512]{2,1,0:T(2,128)(2,1)}, u32[]{:S(2)}) copy-start(bf16[64,1,512]{2,1,0:T(2,128)(2,1)} %copy-done.7) | copy-start | bytes 196612
  106.0 2.7 %copy-start.16 = (bf16[63,1,512]{2,0,1:T(8,128)(2,1)S(1)}, bf16[63,1,512]{2,0,1:T(8,128)(2,1)}, u32[]{:S(2)}) copy-start(bf16[63,1,512]{2,0,1:T(8,128)(2,1)} %copy-done.15) | copy-start | bytes 193540
  106.0 2.7 %copy-start.24 = (bf16[1,512]{1,0:T(2,128)(2,1)S(1)}, bf16[1,512]{1,0:T(2,128)(2,1)}, u32[]{:S(2)}) copy-start(bf16[1,512]{1,0:T(2,128)(2,1)} %copy-done.23) | copy-start | bytes 3076
  110.3 58.7 %reduce-scatter.7.cloned.1.call-start = ((), (), s32[]{:S(2)}) async-start(), calls=%async_computation.3 | async-start | bytes 327680
  110.4 40.1 %collective-permute-start.1 = (bf16[1,512]{1,0:T(2,128)(2,1)S(1)}, bf16[1,512]{1,0:T(2,128)(2,1)S(1)}, u32[]{:S(2)}, u32[]{:S(2)}) collective-permute-start(bf16[1,512]{1,0:T(2,128)(2,1)S(1)} %slice.53), channel_id=1, source_target_pairs={{0,1},{1,2},{2,3},{3,4},{4,5},{5,6},{6,7},{8,9},{9,10},{10,11},{11... | collective-permute-start | bytes 3080 | tf_op jit(solution)/shard_map/ppermute | solution.py:20
  (5 other events, 2.9 us)
Sparse Core Ops, SparseCore 0:
  110.5 38.2 reduce-scatter.4
  151.0 18.0 reduce-scatter.6
where the time goes:
time: 180 us; the launch traced here: 178 us
  blocking collectives  58.6 us (33%)
  waiting for transfers between devices  51.8 us (29%)
  matrix products  22.3 us (12%)
  local copies, waits for them, and re-layouts  21.9 us (12%)
  between operations  14.5 us (8%)
  starting transfers between devices  5.13 us (3%)
  other arithmetic  3.13 us (2%)
    reduce_scatter x1, waiting for transfers between devices, local(): lax.psum_scatter(kernel_terms.astype(jnp.bfloat16), 'ctx', scatter_dimens...  34.7 us
    unnamed x3, waiting for transfers between devices  17.2 us
    all_gather x1, blocking collectives, local(): lax.all_gather(upstream, 'ctx', axis=0, tiled=True)  11.8 us
    all_gather x1, blocking collectives, local(): lax.all_gather(queries, 'ctx', axis=0, tiled=True)  10.4 us
    all_gather x1, blocking collectives, local(): lax.all_gather(keys, 'ctx', axis=0, tiled=True)  9.66 us
    all_gather x1, blocking collectives, local(): lax.all_gather(values, 'ctx', axis=0, tiled=True)  9.66 us
    all_gather x1, blocking collectives, local(): lax.all_gather(jnp.transpose(lse_heads), 'ctx', axis=0, tiled=True)  8.91 us
    all_gather x1, blocking collectives, local(): lax.all_gather(delta_rows, 'ctx', axis=0, tiled=True)  8.18 us
  transfers between devices with their start and end apart: 4, of which 2 were waited for; matrix products, arithmetic and copies ran while one was open for 5% of the time, Pallas kernels for 0%

commit v1 on v0

--- a/solution.py
+++ b/solution.py
@@ -1,8 +1,11 @@
+import functools
 import math
 
 import jax
 import jax.numpy as jnp
 from jax import lax
+from jax.experimental import pallas as pl
+from jax.experimental.pallas import tpu as pltpu
 from jax.sharding import PartitionSpec as P
 
 HEADS = 6
@@ -232,7 +235,371 @@
     return (weight_grad, frame_rows[None])
 
 
+MESH = pl.DeviceIdType.MESH
+ROW_ROW = (((1,), (1,)), ((), ()))
+COL_COL = (((0,), (0,)), ((), ()))
+PAIR = 2 * HEAD_DIM
+
+
+def product(left, right, dims=(((1,), (0,)), ((), ()))):
+    return lax.dot_general(left, right, dims, preferred_element_type=jnp.float32)
+
+
+def normalised(conv_out):
+    activated = 0.5 * conv_out * (1.0 + lax.erf(conv_out * SQRT_HALF))
+    centre = jnp.mean(activated, -1, keepdims=True)
+    spread = jnp.mean((activated - centre) ** 2, -1, keepdims=True)
+    inv_std = lax.rsqrt(spread + EPSILON)
+    return (activated - centre) * inv_std, inv_std
+
+
+def fused(
+    dp_size, ctx_size, count,
+    frames, upstream, conv_hbm, proj_hbm, query_hbm, key_hbm, value_hbm,
+    weight_out, frame_out,
+    taps, cots, conv_w, proj_w, query_w, key_w, value_w,
+    conv_all, q_all, k_all, v_all, stats, grads, cgs, window, z_send, z_recv,
+    load_sem, frame_send, frame_recv, cot_send, cot_recv, stat_send, stat_recv,
+    cg_send, cg_recv, zs_sem, zr_sem,
+):
+    me = lax.axis_index("ctx")
+    record = lax.axis_index("dp")
+    chips = ctx_size // 2
+    chip, core = me // 2, me % 2
+    sibling = chip * 2 + (1 - core)
+    width = frames.shape[1]
+    chan = width // 2
+    total = ctx_size * count
+    own = pl.ds(pl.multiple_of(me * count, count), count)
+
+    def rows_of(index):
+        return pl.ds(pl.multiple_of(index * count, count), count)
+
+    def peer(step):
+        return lax.rem(chip + step, chips) * 2 + core
+
+    loads = []
+    for slot, (source, target) in enumerate(
+        [
+            (frames, taps.at[own, pl.ds(0, width)]),
+            (conv_hbm, conv_w),
+            (proj_hbm, proj_w),
+            (query_hbm, query_w),
+            (key_hbm, key_w),
+            (value_hbm, value_w),
+            (upstream, cots.at[own]),
+        ]
+    ):
+        load = pltpu.make_async_copy(source, target, load_sem.at[slot])
+        load.start()
+        loads.append(load)
+
+    barrier = pltpu.get_barrier_semaphore()
+    for step in range(1, ctx_size):
+        pl.semaphore_signal(
+            barrier, inc=1, device_id=(record, lax.rem(me + step, ctx_size)), device_id_type=MESH
+        )
+    for step in range(1, dp_size):
+        pl.semaphore_signal(
+            barrier, inc=1, device_id=(lax.rem(record + step, dp_size), me), device_id_type=MESH
+        )
+    pl.semaphore_wait(barrier, ctx_size - 1 + dp_size - 1)
+
+    def transfer(view, send, recv, index, target, slot):
+        return pltpu.make_async_remote_copy(
+            src_ref=view(index),
+            dst_ref=view(index),
+            send_sem=send.at[slot],
+            recv_sem=recv.at[index],
+            device_id=(record, target),
+            device_id_type=MESH,
+        )
+
+    def scatter(view, send, recv):
+        copies = []
+        for step in range(1, chips):
+            copies.append(transfer(view, send, recv, me, peer(step), step))
+        copies.append(transfer(view, send, recv, me, sibling, 0))
+        for copy in copies:
+            copy.start()
+        return copies
+
+    def collect(view, send, recv, copies):
+        for step in range(1, chips):
+            source = peer(chips - step)
+            copy = transfer(view, send, recv, source, sibling, chips - 1 + step)
+            copy.wait_recv()
+            copy.start()
+            copies.append(copy)
+        for step in range(chips):
+            source = lax.rem(chip + chips - step, chips) * 2 + (1 - core)
+            transfer(view, send, recv, source, sibling, 0).wait_recv()
+
+    def finish(copies):
+        for copy in copies:
+            copy.wait_send()
+
+    def frame_view(index):
+        return taps.at[rows_of(index), pl.ds(0, width)]
+
+    def cot_view(index):
+        return cots.at[rows_of(index)]
+
+    def cg_view(index):
+        return cgs.at[rows_of(index)]
+
+    loads[0].wait()
+    frame_copies = scatter(frame_view, frame_send, frame_recv)
+    loads[6].wait()
+    cot_copies = scatter(cot_view, cot_send, cot_recv)
+    collect(frame_view, frame_send, frame_recv, frame_copies)
+
+    part = math.gcd(total, 256)
+    last_row = lax.broadcasted_iota(jnp.int32, (total, chan), 0) == total - 1
+    even = taps[:, 0:chan].astype(jnp.float32)
+    taps[:, width : width + chan] = jnp.where(
+        last_row, 0.0, pltpu.roll(even, total - 1, 0)
+    ).astype(jnp.bfloat16)
+    for load in loads[1:6]:
+        load.wait()
+    for start in range(0, total, part):
+        span = slice(start, start + part)
+        conv_out = product(taps[span, :], conv_w[...])
+        conv_all[span, :] = conv_out
+        normed = normalised(conv_out)[0]
+        hidden = product(normed.astype(jnp.bfloat16), proj_w[...]).astype(jnp.bfloat16)
+        q_all[span, :] = product(hidden, query_w[...]).astype(jnp.bfloat16)
+        k_all[span, :] = product(hidden, key_w[...]).astype(jnp.bfloat16)
+        v_all[span, :] = product(hidden, value_w[...]).astype(jnp.bfloat16)
+
+    scale = HEAD_DIM ** (-0.5)
+    lanes = lax.broadcasted_iota(jnp.int32, (count, PAIR), 1)
+    low = (lanes < HEAD_DIM).astype(jnp.float32).astype(jnp.bfloat16)
+    high = (lanes >= HEAD_DIM).astype(jnp.float32).astype(jnp.bfloat16)
+
+    def spread_pair(block):
+        return jnp.concatenate([block * low, block * high], 0)
+
+    def join_pair(square):
+        return jnp.where(lanes < HEAD_DIM, square[:count], square[count:])
+
+    pairs = HEADS // 2
+    features = HEADS * HEAD_DIM
+    stats[me] = jnp.zeros(stats.shape[1:], jnp.float32)
+    saved = []
+    for pair in range(pairs):
+        cols = slice(pair * PAIR, (pair + 1) * PAIR)
+        scores = product(k_all[:, cols], spread_pair(q_all[own, cols]), ROW_ROW) * scale
+        prob_grad = product(v_all[:, cols], spread_pair(cots[own, cols]), ROW_ROW)
+        top = jnp.max(scores, 0, keepdims=True)
+        weights = jnp.exp(scores - top)
+        mass = jnp.sum(weights, 0, keepdims=True)
+        probs = weights / mass
+        delta = jnp.sum(probs * prob_grad, 0, keepdims=True)
+        stats[me, pair : pair + 1, :] = top + jnp.log(mass)
+        stats[me, 4 + pair : 5 + pair, :] = delta
+        saved.append((probs * (prob_grad - delta)).astype(jnp.bfloat16))
+    stat_copies = []
+    for step in range(1, ctx_size):
+        copy = pltpu.make_async_remote_copy(
+            src_ref=stats.at[me],
+            dst_ref=stats.at[me],
+            send_sem=stat_send.at[step],
+            recv_sem=stat_recv.at[me],
+            device_id=(record, lax.rem(me + step, ctx_size)),
+            device_id_type=MESH,
+        )
+        copy.start()
+        stat_copies.append(copy)
+    for pair in range(pairs):
+        cols = slice(pair * PAIR, (pair + 1) * PAIR)
+        square = product(saved[pair], k_all[:, cols], COL_COL)
+        grads[:, cols] = (join_pair(square) * scale).astype(jnp.bfloat16)
+    collect(cot_view, cot_send, cot_recv, cot_copies)
+    first_products = []
+    for pair in range(pairs):
+        cols = slice(pair * PAIR, (pair + 1) * PAIR)
+        first_products.append(
+            (
+                product(spread_pair(k_all[own, cols]), q_all[:, cols], ROW_ROW) * scale,
+                product(spread_pair(v_all[own, cols]), cots[:, cols], ROW_ROW),
+            )
+        )
+    for step in range(1, ctx_size):
+        source = lax.rem(me + step, ctx_size)
+        pltpu.make_async_remote_copy(
+            src_ref=stats.at[source],
+            dst_ref=stats.at[source],
+            send_sem=stat_send.at[step],
+            recv_sem=stat_recv.at[source],
+            device_id=(record, source),
+            device_id_type=MESH,
+        ).wait_recv()
+
+    def along(row):
+        halves = []
+        for start in (0, HEAD_DIM):
+            line = jnp.concatenate(
+                [stats[index, row : row + 1, start : start + count] for index in range(ctx_size)], 1
+            )
+            halves.append(jnp.broadcast_to(line, (count, total)))
+        return jnp.concatenate(halves, 0)
+
+    for pair in range(pairs):
+        cols = slice(pair * PAIR, (pair + 1) * PAIR)
+        scores, prob_grad = first_products[pair]
+        probs = jnp.exp(scores - along(pair))
+        value_square = product(probs.astype(jnp.bfloat16), cots[:, cols])
+        score_grad = (probs * (prob_grad - along(4 + pair))).astype(jnp.bfloat16)
+        key_square = product(score_grad, q_all[:, cols])
+        at_key = features + pair * PAIR
+        at_value = 2 * features + pair * PAIR
+        grads[:, at_key : at_key + PAIR] = (join_pair(key_square) * scale).astype(jnp.bfloat16)
+        grads[:, at_value : at_value + PAIR] = join_pair(value_square).astype(jnp.bfloat16)
+
+    hidden_grad = product(grads[:, 0:features], query_w[...], ROW_ROW)
+    hidden_grad += product(grads[:, features : 2 * features], key_w[...], ROW_ROW)
+    hidden_grad += product(grads[:, 2 * features : 3 * features], value_w[...], ROW_ROW)
+    normed_grad = product(hidden_grad.astype(jnp.bfloat16), proj_w[...], ROW_ROW)
+    conv_out = conv_all[own, :]
+    normed, inv_std = normalised(conv_out)
+    act_grad = inv_std * (
+        normed_grad
+        - jnp.mean(normed_grad, -1, keepdims=True)
+        - normed * jnp.mean(normed_grad * normed, -1, keepdims=True)
+    )
+    conv_grad = (act_grad * gelu_slope(conv_out)).astype(jnp.bfloat16)
+    cgs[own, :] = conv_grad
+    cg_copies = scatter(cg_view, cg_send, cg_recv)
+    frame_out[:, chan:width] = product(
+        conv_grad, conv_w[chan : 2 * chan, :], ROW_ROW
+    ).astype(jnp.bfloat16)
+    even_rows = product(conv_grad, conv_w[0:chan, :], ROW_ROW)
+    collect(cg_view, cg_send, cg_recv, cg_copies)
+
+    share = weight_out.shape[0]
+    columns = weight_out.shape[1]
+    base = (me * share) // 128 * 128
+    picked = taps[:, pl.ds(pl.multiple_of(base, 128), 256)]
+    window[...] = product(picked, cgs[...], COL_COL)
+    shift = me * share - base
+    terms = window[pl.ds(pl.multiple_of(shift, 64), share), :]
+    for index in range(dp_size):
+        z_send[index] = terms[:, index * columns : (index + 1) * columns].astype(jnp.bfloat16)
+    z_copies = []
+    for step in range(1, dp_size):
+        target = lax.rem(record + step, dp_size)
+        copy = pltpu.make_async_remote_copy(
+            src_ref=z_send.at[target],
+            dst_ref=z_recv.at[record],
+            send_sem=zs_sem.at[step],
+            recv_sem=zr_sem.at[record],
+            device_id=(target, me),
+            device_id_type=MESH,
+        )
+        copy.start()
+        z_copies.append(copy)
+    before = lax.rem(me + ctx_size - 1, ctx_size)
+    tail = cgs[pl.ds(pl.multiple_of(before * count + count - 16, 16), 16), :].astype(jnp.float32)
+    incoming = jnp.where(me > 0, tail[15:16, :], 0.0)
+    first_row = lax.broadcasted_iota(jnp.int32, (count, chan), 0) == 0
+    moved = pltpu.roll(cgs[own, :].astype(jnp.float32), 1, 0)
+    moved = jnp.where(first_row, incoming, moved).astype(jnp.bfloat16)
+    even_rows = even_rows + product(moved, conv_w[2 * chan : 3 * chan, :], ROW_ROW)
+    frame_out[:, 0:chan] = even_rows.astype(jnp.bfloat16)
+
+    result = z_send[record].astype(jnp.float32)
+    for step in range(1, dp_size):
+        source = lax.rem(record + step, dp_size)
+        pltpu.make_async_remote_copy(
+            src_ref=z_recv.at[source],
+            dst_ref=z_recv.at[source],
+            send_sem=zs_sem.at[step],
+            recv_sem=zr_sem.at[source],
+            device_id=(source, me),
+            device_id_type=MESH,
+        ).wait_recv()
+        result = result + z_recv[source].astype(jnp.float32)
+    weight_out[...] = result
+    for copies in (frame_copies, cot_copies, stat_copies, cg_copies, z_copies):
+        finish(copies)
+
+
+def local_fused(
+    dp_size, ctx_size,
+    frames, conv_weight, proj_weight, query_weight, key_weight, value_weight, cotangent,
+):
+    inputs = frames[0]
+    count, chan = inputs.shape[0] // 2, inputs.shape[1]
+    total = ctx_size * count
+    depth, features = query_weight.shape
+    share, columns = 3 * chan // ctx_size, chan // dp_size
+    half = jnp.bfloat16
+    dma = pltpu.SemaphoreType.DMA
+    weight_grad, frame_rows = pl.pallas_call(
+        functools.partial(fused, dp_size, ctx_size, count),
+        out_shape=(
+            jax.ShapeDtypeStruct((share, columns), jnp.float32),
+            jax.ShapeDtypeStruct((count, 2 * chan), half),
+        ),
+        in_specs=[pl.BlockSpec(memory_space=pl.ANY)] * 7,
+        out_specs=[pl.BlockSpec(memory_space=pltpu.VMEM)] * 2,
+        scratch_shapes=[
+            pltpu.VMEM((total, 3 * chan), half),
+            pltpu.VMEM((total, features), half),
+            pltpu.VMEM((3 * chan, chan), half),
+            pltpu.VMEM((chan, depth), half),
+            pltpu.VMEM((depth, features), half),
+            pltpu.VMEM((depth, features), half),
+            pltpu.VMEM((depth, features), half),
+            pltpu.VMEM((total, chan), jnp.float32),
+            pltpu.VMEM((total, features), half),
+            pltpu.VMEM((total, features), half),
+            pltpu.VMEM((total, features), half),
+            pltpu.VMEM((ctx_size, 8, PAIR), jnp.float32),
+            pltpu.VMEM((count, 3 * features), half),
+            pltpu.VMEM((total, chan), half),
+            pltpu.VMEM((256, chan), jnp.float32),
+            pltpu.VMEM((dp_size, share, columns), half),
+            pltpu.VMEM((dp_size, share, columns), half),
+            dma((7,)),
+            dma((ctx_size,)),
+            dma((ctx_size,)),
+            dma((ctx_size,)),
+            dma((ctx_size,)),
+            dma((ctx_size,)),
+            dma((ctx_size,)),
+            dma((ctx_size,)),
+            dma((ctx_size,)),
+            dma((dp_size,)),
+            dma((dp_size,)),
+        ],
+        compiler_params=pltpu.CompilerParams(
+            collective_id=0, has_side_effects=True, vmem_limit_bytes=48 * 2**20
+        ),
+    )(
+        inputs.reshape(count, 2 * chan),
+        cotangent[0],
+        conv_weight.reshape(3 * chan, chan),
+        proj_weight,
+        query_weight,
+        key_weight,
+        value_weight,
+    )
+    return weight_grad, frame_rows.reshape(1, 2 * count, chan)
+
+
 def solution(mesh):
     in_specs = (P("dp", "ctx", None), P(), P(), P(), P(), P(), P("dp", "ctx", None))
     out_specs = (P("ctx", "dp"), P("dp", "ctx", None))
-    return jax.shard_map(local, mesh=mesh, in_specs=in_specs, out_specs=out_specs, check_vma=False)
+    dp_size, ctx_size = mesh.shape["dp"], mesh.shape["ctx"]
+
+    def plan(frames, *others):
+        count, chan = frames.shape[1] // 2, frames.shape[2]
+        share = 3 * chan // ctx_size
+        fits = count == HEAD_DIM and ctx_size % 2 == 0 and ctx_size * count <= 512
+        if fits and chan % (128 * dp_size) == 0 and share == 192:
+            return local_fused(dp_size, ctx_size, frames, *others)
+        return local(frames, *others)
+
+    return jax.shard_map(plan, mesh=mesh, in_specs=in_specs, out_specs=out_specs, check_vma=False)

time: 180 us -> 45.6 us (0.25); the launches traced: 178 us -> 45 us
  blocking collectives: 58.6 us -> 0 us
  waiting for transfers between devices: 51.8 us -> 0 us
  Pallas kernels: 0 us -> 35.5 us
  matrix products: 22.3 us -> 0 us
  between operations: 14.5 us -> 0.65 us
  local copies, waits for them, and re-layouts: 21.9 us -> 8.82 us
  starting transfers between devices: 5.13 us -> 0 us
  other arithmetic: 3.13 us -> 0 us
    all_gather x6 -> x0, blocking collectives: 58.6 us -> none  [the longest x1 11.8 us: local(): lax.all_gather(upstream, 'ctx', axis=0, tiled=True)]
    pallas_call x0 -> x1, Pallas kernels: none -> 35.5 us  [local_fused(): pl.pallas_call(functools.partial(fused, dp_size, ctx_size, count), out_sh...]
    reduce_scatter x1 -> x0, waiting for transfers between devices: 34.7 us -> none  [local(): lax.psum_scatter(kernel_terms.astype(jnp.bfloat16), 'ctx', scatter_dimens...]
    dot_general x23 -> x0, matrix products: 22.3 us -> none  [the longest x1 2.32 us: query_block(): jnp.einsum('hqk,khe->qhe', score_grad.astype(jnp.bfloat16), keys_part, pr...]
    unnamed x3 -> x0, waiting for transfers between devices: 17.2 us -> none
    all_gather x6 -> x0, local copies, waits for them, and re-layouts: 5.94 us -> none  [the longest x1 1.92 us: local(): lax.all_gather(values, 'ctx', axis=0, tiled=True)]
    ppermute x2 -> x0, starting transfers between devices: 5.05 us -> none  [from_behind(): lax.ppermute(value, axis, [(source, source + steps) for source in range(i...]
    reshape x4 -> x1, local copies, waits for them, and re-layouts: 5.61 us -> 0.7 us  [local_fused(): return (weight_grad, frame_rows.reshape(1, 2 * count, chan))]
  transfers between devices with their start and end apart: 4 -> 0, of which waited for: 2 -> 0; matrix products, arithmetic and copies ran while one was open for 5% -> 0% of each run, Pallas kernels for 0% -> 0%
where the time goes in v1:
time: 45.6 us; the launch traced here: 45 us
  Pallas kernels  35.5 us (78%)
  local copies, waits for them, and re-layouts  8.82 us (19%)
  between operations  0.65 us (1%)
    pallas_call x1, Pallas kernels, local_fused(): pl.pallas_call(functools.partial(fused, dp_size, ctx_size, count), out_sh...  35.5 us
    unnamed x13, local copies, waits for them, and re-layouts  7.16 us
    another operation x1, local copies, waits for them, and re-layouts, local_fused(): inputs.reshape(count, 2 * chan)  0.95 us

profile of v1, /device:TPU:1, one launch (start us, length us, event | category | flops | bytes accessed | tf_op | source)
XLA Modules:
  0.0 45.0 jit_solution(2844579633135029487)
XLA Ops:
  0.6 1.0 %reshape_squeeze.3.frames = bf16[64,1024]{1,0:T(8,128)(2,1)S(1)} reshape(bf16[1,128,512]{2,1,0:T(8,128)(2,1)} %param.7) | data formatting | bytes 262144 | tf_op jit(solution)/shard_map/reshape;squeeze | solution.py:581
  1.6 0.0 copy-start
  1.6 1.4 %copy-done = bf16[3,512,512]{2,1,0:T(8,128)(2,1)S(1)} copy-done((bf16[3,512,512]{2,1,0:T(8,128)(2,1)S(1)}, bf16[3,512,512]{2,1,0:T(8,128)(2,1)}, u32[]{:S(2)}) %copy-start) | copy-done | bytes 1572888
  3.0 0.0 copy-start.1
  3.0 1.1 %copy-done.1 = bf16[512,768]{1,0:T(8,128)(2,1)S(1)} copy-done((bf16[512,768]{1,0:T(8,128)(2,1)S(1)}, bf16[512,768]{1,0:T(8,128)(2,1)}, u32[]{:S(2)}) %copy-start.1) | copy-done | bytes 786456
  4.1 0.0 copy-start.2
  4.1 1.1 %copy-done.2 = bf16[768,384]{1,0:T(8,128)(2,1)S(1)} copy-done((bf16[768,384]{1,0:T(8,128)(2,1)S(1)}, bf16[768,384]{1,0:T(8,128)(2,1)}, u32[]{:S(2)}) %copy-start.2) | copy-done | bytes 589848
  5.2 0.0 copy-start.3
  5.2 1.1 %copy-done.3 = bf16[768,384]{1,0:T(8,128)(2,1)S(1)} copy-done((bf16[768,384]{1,0:T(8,128)(2,1)S(1)}, bf16[768,384]{1,0:T(8,128)(2,1)}, u32[]{:S(2)}) %copy-start.3) | copy-done | bytes 589848
  6.3 0.0 copy-start.4
  6.3 1.1 %copy-done.4 = bf16[768,384]{1,0:T(8,128)(2,1)S(1)} copy-done((bf16[768,384]{1,0:T(8,128)(2,1)S(1)}, bf16[768,384]{1,0:T(8,128)(2,1)}, u32[]{:S(2)}) %copy-start.4) | copy-done | bytes 589848
  7.3 0.0 copy-start.5
  7.3 0.8 %copy-done.5 = bf16[1,64,384]{2,1,0:T(8,128)(2,1)S(1)} copy-done((bf16[1,64,384]{2,1,0:T(8,128)(2,1)S(1)}, bf16[1,64,384]{2,1,0:T(8,128)(2,1)}, u32[]{:S(2)}) %copy-start.5) | copy-done | bytes 49176
  8.1 35.5 %shard_map.86 = (f32[192,128]{1,0:T(8,128)S(1)}, bf16[64,1024]{1,0:T(8,128)(2,1)S(1)}) custom-call(bf16[64,1024]{1,0:T(8,128)(2,1)S(1)} %reshape_squeeze.3.frames, bf16[64,384]{1,0:T(8,128)(2,1)S(1)} %bitcast.3, bf16[1536,512]{1,0:T(8,128)(2,1)S(1)} %bitcast.2, bf16[512,768]{1,0:T(8,128)(2,1)S(1)} %copy-done.1, bf16[768,384]{1,0:T(8,128)(2,1)S(1)} %copy-done.2, ...), custom_call_target="tpu_custom_call" | custom-call | tf_op jit(solution)/shard_map/pallas_call | solution.py:539
  43.7 0.7 %reshape.11 = bf16[1,128,512]{2,1,0:T(8,128)(2,1)} reshape(bf16[64,1024]{1,0:T(8,128)(2,1)S(1)} %get-tuple-element.5) | data formatting | bytes 262144 | tf_op jit(solution)/shard_map/reshape | solution.py:589
  44.4 0.6 %copy.10 = f32[192,128]{1,0:T(8,128)} copy(f32[192,128]{1,0:T(8,128)S(1)} %get-tuple-element.8) | data formatting | bytes 196608
Async XLA Ops:
  1.6 1.4 %copy-start = (bf16[3,512,512]{2,1,0:T(8,128)(2,1)S(1)}, bf16[3,512,512]{2,1,0:T(8,128)(2,1)}, u32[]{:S(2)}) copy-start(bf16[3,512,512]{2,1,0:T(8,128)(2,1)} %param.8) | copy-start | bytes 4718596
  3.0 1.1 %copy-start.1 = (bf16[512,768]{1,0:T(8,128)(2,1)S(1)}, bf16[512,768]{1,0:T(8,128)(2,1)}, u32[]{:S(2)}) copy-start(bf16[512,768]{1,0:T(8,128)(2,1)} %proj_hbm.1) | copy-start | bytes 2359300
  4.1 1.1 %copy-start.2 = (bf16[768,384]{1,0:T(8,128)(2,1)S(1)}, bf16[768,384]{1,0:T(8,128)(2,1)}, u32[]{:S(2)}) copy-start(bf16[768,384]{1,0:T(8,128)(2,1)} %query_hbm.1) | copy-start | bytes 1769476
  5.2 1.1 %copy-start.3 = (bf16[768,384]{1,0:T(8,128)(2,1)S(1)}, bf16[768,384]{1,0:T(8,128)(2,1)}, u32[]{:S(2)}) copy-start(bf16[768,384]{1,0:T(8,128)(2,1)} %key_hbm.1) | copy-start | bytes 1769476
  6.3 1.1 %copy-start.4 = (bf16[768,384]{1,0:T(8,128)(2,1)S(1)}, bf16[768,384]{1,0:T(8,128)(2,1)}, u32[]{:S(2)}) copy-start(bf16[768,384]{1,0:T(8,128)(2,1)} %value_hbm.1) | copy-start | bytes 1769476
  7.3 0.8 %copy-start.5 = (bf16[1,64,384]{2,1,0:T(8,128)(2,1)S(1)}, bf16[1,64,384]{2,1,0:T(8,128)(2,1)}, u32[]{:S(2)}) copy-start(bf16[1,64,384]{2,1,0:T(8,128)(2,1)} %param.13) | copy-start | bytes 147460

commit v2 on v1

--- a/solution.py
+++ b/solution.py
@@ -239,6 +239,7 @@
 ROW_ROW = (((1,), (1,)), ((), ()))
 COL_COL = (((0,), (0,)), ((), ()))
 PAIR = 2 * HEAD_DIM
+GROUP = 2
 
 
 def product(left, right, dims=(((1,), (0,)), ((), ()))):
@@ -318,22 +319,28 @@
     def scatter(view, send, recv):
         copies = []
         for step in range(1, chips):
-            copies.append(transfer(view, send, recv, me, peer(step), step))
+            copies.append(transfer(view, send, recv, me, peer(chips - step), step))
         copies.append(transfer(view, send, recv, me, sibling, 0))
         for copy in copies:
             copy.start()
         return copies
 
+    def pass_on(view, send, recv, copies, step):
+        source = peer(step)
+        copy = transfer(view, send, recv, source, sibling, chips - 1 + step)
+        copy.wait_recv()
+        copy.start()
+        copies.append(copy)
+
+    def arrive(view, send, recv, step):
+        source = lax.rem(chip + step, chips) * 2 + (1 - core)
+        transfer(view, send, recv, source, sibling, 0).wait_recv()
+
     def collect(view, send, recv, copies):
         for step in range(1, chips):
-            source = peer(chips - step)
-            copy = transfer(view, send, recv, source, sibling, chips - 1 + step)
-            copy.wait_recv()
-            copy.start()
-            copies.append(copy)
+            pass_on(view, send, recv, copies, step)
         for step in range(chips):
-            source = lax.rem(chip + chips - step, chips) * 2 + (1 - core)
-            transfer(view, send, recv, source, sibling, 0).wait_recv()
+            arrive(view, send, recv, step)
 
     def finish(copies):
         for copy in copies:
@@ -345,32 +352,60 @@
     def cot_view(index):
         return cots.at[rows_of(index)]
 
-    def cg_view(index):
-        return cgs.at[rows_of(index)]
+    def cg_view(half):
+        return lambda index: cgs.at[rows_of(index), pl.ds(half * (chan // 2), chan // 2)]
 
     loads[0].wait()
     frame_copies = scatter(frame_view, frame_send, frame_recv)
     loads[6].wait()
     cot_copies = scatter(cot_view, cot_send, cot_recv)
-    collect(frame_view, frame_send, frame_recv, frame_copies)
-
-    part = math.gcd(total, 256)
-    last_row = lax.broadcasted_iota(jnp.int32, (total, chan), 0) == total - 1
-    even = taps[:, 0:chan].astype(jnp.float32)
-    taps[:, width : width + chan] = jnp.where(
-        last_row, 0.0, pltpu.roll(even, total - 1, 0)
-    ).astype(jnp.bfloat16)
+    pair_rows = 2 * count
+    last_row = lax.broadcasted_iota(jnp.int32, (pair_rows, chan), 0) == pair_rows - 1
+
+    def pair_span(index):
+        return pl.ds(pl.multiple_of(index * pair_rows, pair_rows), pair_rows)
+
+    def forward(steps):
+        spans = []
+        for step in steps:
+            here = lax.rem(chip + step, chips)
+            after = lax.rem(here + 1, chips)
+            span = pair_span(here)
+            even = taps[span, 0:chan].astype(jnp.float32)
+            head = taps[pl.ds(pl.multiple_of(after * pair_rows, 16), 16), 0:chan]
+            following = jnp.where(here < chips - 1, head.astype(jnp.float32)[0:1, :], 0.0)
+            taps[span, width : width + chan] = jnp.where(
+                last_row, following, pltpu.roll(even, pair_rows - 1, 0)
+            ).astype(jnp.bfloat16)
+            spans.append(span)
+        block = jnp.concatenate([taps[span, :] for span in spans], 0)
+        conv_out = product(block, conv_w[...])
+        normed = normalised(conv_out)[0]
+        hidden = product(normed.astype(jnp.bfloat16), proj_w[...]).astype(jnp.bfloat16)
+        queries = product(hidden, query_w[...]).astype(jnp.bfloat16)
+        keys = product(hidden, key_w[...]).astype(jnp.bfloat16)
+        values = product(hidden, value_w[...]).astype(jnp.bfloat16)
+        for place, span in enumerate(spans):
+            piece = slice(place * pair_rows, (place + 1) * pair_rows)
+            conv_all[span, :] = conv_out[piece]
+            q_all[span, :] = queries[piece]
+            k_all[span, :] = keys[piece]
+            v_all[span, :] = values[piece]
+
     for load in loads[1:6]:
         load.wait()
-    for start in range(0, total, part):
-        span = slice(start, start + part)
-        conv_out = product(taps[span, :], conv_w[...])
-        conv_all[span, :] = conv_out
-        normed = normalised(conv_out)[0]
-        hidden = product(normed.astype(jnp.bfloat16), proj_w[...]).astype(jnp.bfloat16)
-        q_all[span, :] = product(hidden, query_w[...]).astype(jnp.bfloat16)
-        k_all[span, :] = product(hidden, key_w[...]).astype(jnp.bfloat16)
-        v_all[span, :] = product(hidden, value_w[...]).astype(jnp.bfloat16)
+    arrive(frame_view, frame_send, frame_recv, 0)
+    waiting = []
+    for step in range(1, chips + 2):
+        if step < chips:
+            pass_on(frame_view, frame_send, frame_recv, frame_copies, step)
+        if 1 < step <= chips:
+            arrive(frame_view, frame_send, frame_recv, step - 1)
+        if step > 1:
+            waiting.append(step - 2)
+        if len(waiting) == GROUP or (waiting and step == chips + 1):
+            forward(waiting)
+            waiting = []
 
     scale = HEAD_DIM ** (-0.5)
     lanes = lax.broadcasted_iota(jnp.int32, (count, PAIR), 1)
@@ -470,35 +505,42 @@
     )
     conv_grad = (act_grad * gelu_slope(conv_out)).astype(jnp.bfloat16)
     cgs[own, :] = conv_grad
-    cg_copies = scatter(cg_view, cg_send, cg_recv)
+    cg_parts = [
+        scatter(cg_view(half), cg_send.at[half], cg_recv.at[half]) for half in range(2)
+    ]
     frame_out[:, chan:width] = product(
         conv_grad, conv_w[chan : 2 * chan, :], ROW_ROW
     ).astype(jnp.bfloat16)
     even_rows = product(conv_grad, conv_w[0:chan, :], ROW_ROW)
-    collect(cg_view, cg_send, cg_recv, cg_copies)
-
     share = weight_out.shape[0]
     columns = weight_out.shape[1]
     base = (me * share) // 128 * 128
+    shift = pl.multiple_of(me * share - base, 64)
     picked = taps[:, pl.ds(pl.multiple_of(base, 128), 256)]
-    window[...] = product(picked, cgs[...], COL_COL)
-    shift = me * share - base
-    terms = window[pl.ds(pl.multiple_of(shift, 64), share), :]
-    for index in range(dp_size):
-        z_send[index] = terms[:, index * columns : (index + 1) * columns].astype(jnp.bfloat16)
-    z_copies = []
-    for step in range(1, dp_size):
-        target = lax.rem(record + step, dp_size)
-        copy = pltpu.make_async_remote_copy(
-            src_ref=z_send.at[target],
+
+    def z_copy(index):
+        return pltpu.make_async_remote_copy(
+            src_ref=z_send.at[index],
             dst_ref=z_recv.at[record],
-            send_sem=zs_sem.at[step],
+            send_sem=zs_sem.at[index],
             recv_sem=zr_sem.at[record],
-            device_id=(target, me),
+            device_id=(index, me),
             device_id_type=MESH,
         )
-        copy.start()
-        z_copies.append(copy)
+
+    for half in range(2):
+        collect(cg_view(half), cg_send.at[half], cg_recv.at[half], cg_parts[half])
+        side = slice(half * (chan // 2), (half + 1) * (chan // 2))
+        window[:, side] = product(picked, cgs[:, side], COL_COL)
+        for index in range(half * dp_size // 2, (half + 1) * dp_size // 2):
+            z_send[index] = window[
+                pl.ds(shift, share), index * columns : (index + 1) * columns
+            ].astype(jnp.bfloat16)
+
+            @pl.when(record != index)
+            def _():
+                z_copy(index).start()
+
     before = lax.rem(me + ctx_size - 1, ctx_size)
     tail = cgs[pl.ds(pl.multiple_of(before * count + count - 16, 16), 16), :].astype(jnp.float32)
     incoming = jnp.where(me > 0, tail[15:16, :], 0.0)
@@ -514,15 +556,20 @@
         pltpu.make_async_remote_copy(
             src_ref=z_recv.at[source],
             dst_ref=z_recv.at[source],
-            send_sem=zs_sem.at[step],
+            send_sem=zs_sem.at[source],
             recv_sem=zr_sem.at[source],
             device_id=(source, me),
             device_id_type=MESH,
         ).wait_recv()
         result = result + z_recv[source].astype(jnp.float32)
     weight_out[...] = result
-    for copies in (frame_copies, cot_copies, stat_copies, cg_copies, z_copies):
+    for copies in (frame_copies, cot_copies, stat_copies, cg_parts[0], cg_parts[1]):
         finish(copies)
+    for index in range(dp_size):
+
+        @pl.when(record != index)
+        def _():
+            z_copy(index).wait_send()
 
 
 def local_fused(
@@ -542,7 +589,7 @@
             jax.ShapeDtypeStruct((share, columns), jnp.float32),
             jax.ShapeDtypeStruct((count, 2 * chan), half),
         ),
-        in_specs=[pl.BlockSpec(memory_space=pl.ANY)] * 7,
+        in_specs=[pl.BlockSpec(memory_space=pltpu.HBM)] * 7,
         out_specs=[pl.BlockSpec(memory_space=pltpu.VMEM)] * 2,
         scratch_shapes=[
             pltpu.VMEM((total, 3 * chan), half),
@@ -569,13 +616,13 @@
             dma((ctx_size,)),
             dma((ctx_size,)),
             dma((ctx_size,)),
-            dma((ctx_size,)),
-            dma((ctx_size,)),
+            dma((2, ctx_size)),
+            dma((2, ctx_size)),
             dma((dp_size,)),
             dma((dp_size,)),
         ],
         compiler_params=pltpu.CompilerParams(
-            collective_id=0, has_side_effects=True, vmem_limit_bytes=48 * 2**20
+            collective_id=0, has_side_effects=True, vmem_limit_bytes=60 * 2**20
         ),
     )(
         inputs.reshape(count, 2 * chan),
@@ -598,7 +645,7 @@
         count, chan = frames.shape[1] // 2, frames.shape[2]
         share = 3 * chan // ctx_size
         fits = count == HEAD_DIM and ctx_size % 2 == 0 and ctx_size * count <= 512
-        if fits and chan % (128 * dp_size) == 0 and share == 192:
+        if fits and chan % (128 * dp_size) == 0 and share == 192 and dp_size % 2 == 0:
             return local_fused(dp_size, ctx_size, frames, *others)
         return local(frames, *others)
 

time: 45.6 us -> 40.4 us (0.89)
  local copies, waits for them, and re-layouts: 8.82 us -> 4.75 us
  Pallas kernels: 35.5 us -> 34.8 us
    unnamed x13 -> x1, local copies, waits for them, and re-layouts: 7.16 us -> 1.54 us
    reshape x1, local copies, waits for them, and re-layouts: 0.7 us -> 1.61 us  [local_fused(): return (weight_grad, frame_rows.reshape(1, 2 * count, chan))]
    pallas_call x1, Pallas kernels: 35.5 us -> 34.8 us  [local_fused(): pl.pallas_call(functools.partial(fused, dp_size, ctx_size, count), out_sh...]
    another operation x1, local copies, waits for them, and re-layouts: 0.95 us -> 1.61 us  [local_fused(): inputs.reshape(count, 2 * chan)]
where the time goes in v2:
time: 40.4 us; the launch traced here: 40.2 us
  Pallas kernels  34.8 us (86%)
  local copies, waits for them, and re-layouts  4.75 us (12%)
  between operations  0.64 us (2%)
    pallas_call x1, Pallas kernels, local_fused(): pl.pallas_call(functools.partial(fused, dp_size, ctx_size, count), out_sh...  34.8 us
    reshape x1, local copies, waits for them, and re-layouts, local_fused(): return (weight_grad, frame_rows.reshape(1, 2 * count, chan))  1.61 us
    another operation x1, local copies, waits for them, and re-layouts, local_fused(): inputs.reshape(count, 2 * chan)  1.61 us
    unnamed x1, local copies, waits for them, and re-layouts  1.54 us

profile of v2, /device:TPU:1, one launch (start us, length us, event | category | flops | bytes accessed | tf_op | source)
XLA Modules:
  0.0 40.2 jit_solution(12612063979743948330)
XLA Ops:
  0.6 1.6 %reshape_squeeze.3.frames = bf16[64,1024]{1,0:T(8,128)(2,1)} reshape(bf16[1,128,512]{2,1,0:T(8,128)(2,1)} %param.7) | data formatting | bytes 262144 | tf_op jit(solution)/shard_map/reshape;squeeze | solution.py:628
  2.2 34.8 %shard_map.86 = (f32[192,128]{1,0:T(8,128)}, bf16[64,1024]{1,0:T(8,128)(2,1)}) custom-call(bf16[64,1024]{1,0:T(8,128)(2,1)} %reshape_squeeze.3.frames, bf16[64,384]{1,0:T(8,128)(2,1)} %bitcast.3, bf16[1536,512]{1,0:T(8,128)(2,1)} %bitcast.2, bf16[512,768]{1,0:T(8,128)(2,1)} %proj_hbm.1, bf16[768,384]{1,0:T(8,128)(2,1)} %query_hbm.1, ...), custom_call_target="tpu_custom_call" | custom-call | tf_op jit(solution)/shard_map/pallas_call | solution.py:586
  37.1 1.6 %reshape.11 = bf16[1,128,512]{2,1,0:T(8,128)(2,1)} reshape(bf16[64,1024]{1,0:T(8,128)(2,1)} %get-tuple-element.5) | data formatting | bytes 262144 | tf_op jit(solution)/shard_map/reshape | solution.py:636
  38.7 1.5 %copy.10 = f32[192,128]{1,0:T(8,128)} copy(f32[192,128]{1,0:T(8,128)} %get-tuple-element.8) | data formatting | bytes 196608

commit v3 on v2

--- a/solution.py
+++ b/solution.py
@@ -357,8 +357,6 @@
 
     loads[0].wait()
     frame_copies = scatter(frame_view, frame_send, frame_recv)
-    loads[6].wait()
-    cot_copies = scatter(cot_view, cot_send, cot_recv)
     pair_rows = 2 * count
     last_row = lax.broadcasted_iota(jnp.int32, (pair_rows, chan), 0) == pair_rows - 1
 
@@ -403,6 +401,9 @@
             arrive(frame_view, frame_send, frame_recv, step - 1)
         if step > 1:
             waiting.append(step - 2)
+        if step == chips - 1:
+            loads[6].wait()
+            cot_copies = scatter(cot_view, cot_send, cot_recv)
         if len(waiting) == GROUP or (waiting and step == chips + 1):
             forward(waiting)
             waiting = []
@@ -644,7 +645,7 @@
     def plan(frames, *others):
         count, chan = frames.shape[1] // 2, frames.shape[2]
         share = 3 * chan // ctx_size
-        fits = count == HEAD_DIM and ctx_size % 2 == 0 and ctx_size * count <= 512
+        fits = count == HEAD_DIM and ctx_size % 2 == 0 and ctx_size > 2 and ctx_size * count <= 512
         if fits and chan % (128 * dp_size) == 0 and share == 192 and dp_size % 2 == 0:
             return local_fused(dp_size, ctx_size, frames, *others)
         return local(frames, *others)

time: 40.4 us -> 39.3 us (0.973)
  Pallas kernels: 34.8 us -> 33.7 us
    pallas_call x1, Pallas kernels: 34.8 us -> 33.7 us  [local_fused(): pl.pallas_call(functools.partial(fused, dp_size, ctx_size, count), out_sh...]
where the time goes in v3:
time: 39.3 us; the launch traced here: 39.1 us
  Pallas kernels  33.7 us (86%)
  local copies, waits for them, and re-layouts  4.75 us (12%)
  between operations  0.64 us (2%)
    pallas_call x1, Pallas kernels, local_fused(): pl.pallas_call(functools.partial(fused, dp_size, ctx_size, count), out_sh...  33.7 us
    reshape x1, local copies, waits for them, and re-layouts, local_fused(): return (weight_grad, frame_rows.reshape(1, 2 * count, chan))  1.61 us
    another operation x1, local copies, waits for them, and re-layouts, local_fused(): inputs.reshape(count, 2 * chan)  1.61 us
    unnamed x1, local copies, waits for them, and re-layouts  1.54 us

profile of v3, /device:TPU:1, one launch (start us, length us, event | category | flops | bytes accessed | tf_op | source)
XLA Modules:
  0.0 39.1 jit_solution(16980031772523984319)
XLA Ops:
  0.6 1.6 %reshape_squeeze.3.frames = bf16[64,1024]{1,0:T(8,128)(2,1)} reshape(bf16[1,128,512]{2,1,0:T(8,128)(2,1)} %param.7) | data formatting | bytes 262144 | tf_op jit(solution)/shard_map/reshape;squeeze | solution.py:629
  2.2 33.7 %shard_map.86 = (f32[192,128]{1,0:T(8,128)}, bf16[64,1024]{1,0:T(8,128)(2,1)}) custom-call(bf16[64,1024]{1,0:T(8,128)(2,1)} %reshape_squeeze.3.frames, bf16[64,384]{1,0:T(8,128)(2,1)} %bitcast.3, bf16[1536,512]{1,0:T(8,128)(2,1)} %bitcast.2, bf16[512,768]{1,0:T(8,128)(2,1)} %proj_hbm.1, bf16[768,384]{1,0:T(8,128)(2,1)} %query_hbm.1, ...), custom_call_target="tpu_custom_call" | custom-call | tf_op jit(solution)/shard_map/pallas_call | solution.py:587
  35.9 1.6 %reshape.11 = bf16[1,128,512]{2,1,0:T(8,128)(2,1)} reshape(bf16[64,1024]{1,0:T(8,128)(2,1)} %get-tuple-element.5) | data formatting | bytes 262144 | tf_op jit(solution)/shard_map/reshape | solution.py:637
  37.5 1.5 %copy.10 = f32[192,128]{1,0:T(8,128)} copy(f32[192,128]{1,0:T(8,128)} %get-tuple-element.8) | data formatting | bytes 196608

commit v4 on v3

--- a/solution.py
+++ b/solution.py
@@ -239,7 +239,7 @@
 ROW_ROW = (((1,), (1,)), ((), ()))
 COL_COL = (((0,), (0,)), ((), ()))
 PAIR = 2 * HEAD_DIM
-GROUP = 2
+GROUP = 1
 
 
 def product(left, right, dims=(((1,), (0,)), ((), ()))):
@@ -512,7 +512,6 @@
     frame_out[:, chan:width] = product(
         conv_grad, conv_w[chan : 2 * chan, :], ROW_ROW
     ).astype(jnp.bfloat16)
-    even_rows = product(conv_grad, conv_w[0:chan, :], ROW_ROW)
     share = weight_out.shape[0]
     columns = weight_out.shape[1]
     base = (me * share) // 128 * 128
@@ -548,6 +547,7 @@
     first_row = lax.broadcasted_iota(jnp.int32, (count, chan), 0) == 0
     moved = pltpu.roll(cgs[own, :].astype(jnp.float32), 1, 0)
     moved = jnp.where(first_row, incoming, moved).astype(jnp.bfloat16)
+    even_rows = product(conv_grad, conv_w[0:chan, :], ROW_ROW)
     even_rows = even_rows + product(moved, conv_w[2 * chan : 3 * chan, :], ROW_ROW)
     frame_out[:, 0:chan] = even_rows.astype(jnp.bfloat16)
 

time: 39.3 us -> 39.4 us (level)
  no operation moved by 1% of the time
where the time goes in v4:
time: 39.4 us; the launch traced here: 39.2 us
  Pallas kernels  33.8 us (86%)
  local copies, waits for them, and re-layouts  4.75 us (12%)
  between operations  0.64 us (2%)
    pallas_call x1, Pallas kernels, local_fused(): pl.pallas_call(functools.partial(fused, dp_size, ctx_size, count), out_sh...  33.8 us
    reshape x1, local copies, waits for them, and re-layouts, local_fused(): return (weight_grad, frame_rows.reshape(1, 2 * count, chan))  1.61 us
    another operation x1, local copies, waits for them, and re-layouts, local_fused(): inputs.reshape(count, 2 * chan)  1.61 us
    unnamed x1, local copies, waits for them, and re-layouts  1.54 us

profile of v4, /device:TPU:1, one launch (start us, length us, event | category | flops | bytes accessed | tf_op | source)
XLA Modules:
  0.0 39.2 jit_solution(8773855144008276491)
XLA Ops:
  0.6 1.6 %reshape_squeeze.3.frames = bf16[64,1024]{1,0:T(8,128)(2,1)} reshape(bf16[1,128,512]{2,1,0:T(8,128)(2,1)} %param.7) | data formatting | bytes 262144 | tf_op jit(solution)/shard_map/reshape;squeeze | solution.py:629
  2.2 33.8 %shard_map.86 = (f32[192,128]{1,0:T(8,128)}, bf16[64,1024]{1,0:T(8,128)(2,1)}) custom-call(bf16[64,1024]{1,0:T(8,128)(2,1)} %reshape_squeeze.3.frames, bf16[64,384]{1,0:T(8,128)(2,1)} %bitcast.3, bf16[1536,512]{1,0:T(8,128)(2,1)} %bitcast.2, bf16[512,768]{1,0:T(8,128)(2,1)} %proj_hbm.1, bf16[768,384]{1,0:T(8,128)(2,1)} %query_hbm.1, ...), custom_call_target="tpu_custom_call" | custom-call | tf_op jit(solution)/shard_map/pallas_call | solution.py:587
  36.0 1.6 %reshape.11 = bf16[1,128,512]{2,1,0:T(8,128)(2,1)} reshape(bf16[64,1024]{1,0:T(8,128)(2,1)} %get-tuple-element.5) | data formatting | bytes 262144 | tf_op jit(solution)/shard_map/reshape | solution.py:637
  37.6 1.5 %copy.10 = f32[192,128]{1,0:T(8,128)} copy(f32[192,128]{1,0:T(8,128)} %get-tuple-element.8) | data formatting | bytes 196608
